TPU v7x, 128 devices: a whole 4x4x4 slice. The times are simulated.
128 devices in a mesh: win: 4 (over y_lo, core), blk: 32 (over y_hi, z, x).
Axes of the slice: x: 4, y: 4 (y_hi: 2, y_lo: 2; y = y_hi * 2 + y_lo), z: 4, core: 2. Of those that a mesh axis runs over, the one named last changes fastest.
Arguments:
- hidden_in: bfloat16 [4, 8192, 1920], P('win', 'blk'), may hold values from -6 to 6
- cond_codes: int32 [4, 2048], P('win', 'blk'), may hold values from 0 to 2047
- level_ids: int32 [4], P('win'), may hold values from 0 to 1, as said below
- qkv_weight: bfloat16 [1920, 1440], P(('win', 'blk')), may hold values from -0.125 to 0.125
- attn_out_weight: bfloat16 [480, 1920], P(None, ('win', 'blk')), may hold values from -1 to 1
- mlp_in_weight: bfloat16 [1920, 1920], P(('win', 'blk')), may hold values from -0.125 to 0.125
- mlp_out_weight: bfloat16 [1920, 1920], P(('win', 'blk')), may hold values from -0.125 to 0.125
- code_table: bfloat16 [2048, 1920], P(('win', 'blk')), may hold values from -6 to 6
- level_table: bfloat16 [2, 1920], P(None, ('win', 'blk')), may hold values from -6 to 6
- norm_gain: bfloat16 [2, 1920], P(None, ('win', 'blk')), may hold values from 0.5 to 2
- norm_bias: bfloat16 [2, 1920], P(None, ('win', 'blk')), may hold values from -0.5 to 0.5
- grad_out: bfloat16 [4, 8192, 1920], P('win', 'blk'), may hold values from -6 to 6
Outputs:
- block_out: bfloat16 [4, 8192, 1920], P('win', 'blk')
- grad_in: float32 [4, 8192, 1920], P('win', 'blk')
- grad_qkv: float32 [1920, 1440], P(('win', 'blk'))
- grad_attn_out: float32 [480, 1920], P(None, ('win', 'blk'))
- grad_mlp_in: float32 [1920, 1920], P(('win', 'blk'))
- grad_mlp_out: float32 [1920, 1920], P(('win', 'blk'))
- grad_codes: float32 [2048, 1920], P(('win', 'blk'))
- grad_levels: float32 [2, 1920], P(None, ('win', 'blk'))
- grad_gain: float32 [2, 1920], P(None, ('win', 'blk'))
- grad_bias: float32 [2, 1920], P(None, ('win', 'blk'))
Inputs may be any that keep to these rules, and one draw needn't show every extreme that they name: `level_ids`: each level is the level of 2 windows.
All inputs are finite; a program needn't handle non-finite values.
Results may differ from a plain program's by a relative error of at most 0.0092.
Values may be sent and summed in bfloat16 or wider, within the bound.
No kernel may reach another device: no remote copies, remote signals or barrier semaphores. Data moves between devices by JAX's collectives and lax.ppermute only.
A program may use at most 192 MiB of HBM per device.

v0:
```python
import jax
import jax.numpy as jnp
from jax import lax
from jax.sharding import PartitionSpec as P

HEADS = 1
HEAD = 480
VOCAB = 2048
BLOCK = 128
RATIO = 4


epsilon = 1e-05


def layer_norm(stream, gain, shift):
    average = jnp.mean(stream, axis=-1, keepdims=True)
    centered = stream - average
    variance = jnp.mean(centered * centered, axis=-1, keepdims=True)
    return centered * lax.rsqrt(variance + epsilon) * gain + shift


def contract_rows(left, right):
    return lax.dot_general(
        left, right, (((0,), (0,)), ((), ())), preferred_element_type=jnp.float32
    )


def contract_cols(left, right):
    return lax.dot_general(
        left, right, (((1,), (1,)), ((), ())), preferred_element_type=jnp.float32
    )


def attend_scores(query_part, key_part):
    blocks = query_part.shape[0]
    scores = jnp.einsum(
        "ichd,jchd->chij", query_part, key_part, preferred_element_type=jnp.float32
    ) * HEAD ** (-0.5)
    causal = jnp.arange(blocks)[:, None] >= jnp.arange(blocks)[None, :]
    return jnp.where(causal, scores, -1e30)


def body(
    hidden_in,
    cond_codes,
    level_ids,
    qkv_weight,
    attn_out_weight,
    mlp_in_weight,
    mlp_out_weight,
    code_table,
    level_table,
    norm_gain,
    norm_bias,
    grad_out,
):
    gathered = (
        lax.all_gather(qkv_weight, ("win", "blk"), axis=0, tiled=True),
        lax.all_gather(attn_out_weight, ("win", "blk"), axis=1, tiled=True),
        lax.all_gather(mlp_in_weight, ("win", "blk"), axis=0, tiled=True),
        lax.all_gather(mlp_out_weight, ("win", "blk"), axis=0, tiled=True),
        lax.all_gather(code_table, ("win", "blk"), axis=0, tiled=True),
        lax.all_gather(level_table, ("win", "blk"), axis=1, tiled=True),
        lax.all_gather(norm_gain, ("win", "blk"), axis=1, tiled=True),
        lax.all_gather(norm_bias, ("win", "blk"), axis=1, tiled=True),
    )
    qkv_full, attn_full, expand_full, reduce_full, table_full, level_full, gain_full, shift_full = (
        gathered
    )
    gain_rows = gain_full.astype(jnp.float32)
    shifts = shift_full.astype(jnp.float32)
    hidden = hidden_in[0].astype(jnp.float32)
    tokens = hidden.shape[0]
    blk_here = tokens // BLOCK
    looked = jnp.take(table_full, cond_codes[0], axis=0).astype(jnp.float32)
    embedded = jnp.repeat(looked, RATIO, axis=0)
    chosen = jnp.arange(level_full.shape[0]) == level_ids[0]
    level_row = jnp.sum(jnp.where(chosen[:, None], level_full.astype(jnp.float32), 0.0), axis=0)
    stream = hidden + embedded + level_row[None, :]
    normed_first = layer_norm(stream, gain_rows[0], shifts[0]).astype(jnp.bfloat16)
    packed = jnp.dot(normed_first, qkv_full, preferred_element_type=jnp.float32).astype(
        jnp.bfloat16
    )
    packed_cols = lax.all_to_all(
        packed.reshape(blk_here, BLOCK, -1), "blk", split_axis=1, concat_axis=0, tiled=True
    )
    blocks, columns = (packed_cols.shape[0], packed_cols.shape[1])
    head_parts = packed_cols.reshape(blocks, columns, 3, HEADS, HEAD)
    query_part = head_parts[:, :, 0]
    key_part = head_parts[:, :, 1]
    value_part = head_parts[:, :, 2]
    scores = attend_scores(query_part, key_part)
    row_top = jnp.max(scores, axis=-1, keepdims=True)
    log_total = row_top + jnp.log(jnp.sum(jnp.exp(scores - row_top), axis=-1, keepdims=True))
    probs_low = jnp.exp(scores - log_total).astype(jnp.bfloat16)
    mixed_cols = jnp.einsum(
        "chij,jchd->ichd", probs_low, value_part, preferred_element_type=jnp.float32
    ).astype(jnp.bfloat16)
    mixed = lax.all_to_all(
        mixed_cols.reshape(blocks, columns, -1), "blk", split_axis=0, concat_axis=1, tiled=True
    ).reshape(tokens, -1)
    stream_mid = stream + jnp.dot(mixed, attn_full, preferred_element_type=jnp.float32)
    normed_second = layer_norm(stream_mid, gain_rows[1], shifts[1]).astype(jnp.bfloat16)
    upward = jnp.dot(normed_second, expand_full, preferred_element_type=jnp.float32)
    active = jax.nn.gelu(upward, approximate=True).astype(jnp.bfloat16)
    block_out = (
        stream_mid + jnp.dot(active, reduce_full, preferred_element_type=jnp.float32)
    ).astype(jnp.bfloat16)
    qkv_back, attn_back, expand_back, reduce_back, gain_back = (
        lax.all_gather(qkv_weight, ("win", "blk"), axis=0, tiled=True),
        lax.all_gather(attn_out_weight, ("win", "blk"), axis=1, tiled=True),
        lax.all_gather(mlp_in_weight, ("win", "blk"), axis=0, tiled=True),
        lax.all_gather(mlp_out_weight, ("win", "blk"), axis=0, tiled=True),
        lax.all_gather(norm_gain, ("win", "blk"), axis=1, tiled=True),
    )
    gains_back = gain_back.astype(jnp.float32)
    upstream = grad_out[0]
    cotangent = upstream.astype(jnp.float32)
    grad_reduce = contract_rows(active, upstream)
    d_active = contract_cols(upstream, reduce_back)
    _, gelu_pull = jax.vjp(lambda pre_act: jax.nn.gelu(pre_act, approximate=True), upward)
    d_upward = gelu_pull(d_active)[0].astype(jnp.bfloat16)
    grad_expand = contract_rows(normed_second, d_upward)
    d_normed_second = contract_cols(d_upward, expand_back)
    _, second_pull = jax.vjp(layer_norm, stream_mid, gains_back[1], shifts[1])
    d_stream_part, d_gain_second, d_shift_second = second_pull(d_normed_second)
    d_stream_mid = cotangent + d_stream_part
    d_attn = d_stream_mid.astype(jnp.bfloat16)
    grad_attn = contract_rows(mixed, d_attn)
    d_mixed = contract_cols(d_attn, attn_back).astype(jnp.bfloat16)
    d_mixed_cols = lax.all_to_all(
        d_mixed.reshape(blk_here, BLOCK, -1), "blk", split_axis=1, concat_axis=0, tiled=True
    ).reshape(blocks, columns, HEADS, HEAD)
    probs_again = jnp.exp(attend_scores(query_part, key_part) - log_total)
    probs_round = probs_again.astype(jnp.bfloat16)
    d_values = jnp.einsum(
        "chij,ichd->jchd", probs_round, d_mixed_cols, preferred_element_type=jnp.float32
    )
    d_probs = jnp.einsum(
        "ichd,jchd->chij", d_mixed_cols, value_part, preferred_element_type=jnp.float32
    )
    d_scores = (
        probs_again * (d_probs - jnp.sum(probs_again * d_probs, axis=-1, keepdims=True))
    ).astype(jnp.bfloat16)
    d_queries = jnp.einsum(
        "chij,jchd->ichd", d_scores, key_part, preferred_element_type=jnp.float32
    ) * HEAD ** (-0.5)
    d_keys = jnp.einsum(
        "chij,ichd->jchd", d_scores, query_part, preferred_element_type=jnp.float32
    ) * HEAD ** (-0.5)
    d_parts = (
        jnp.stack((d_queries, d_keys, d_values), axis=2)
        .astype(jnp.bfloat16)
        .reshape(blocks, columns, -1)
    )
    d_packed = lax.all_to_all(d_parts, "blk", split_axis=0, concat_axis=1, tiled=True).reshape(
        tokens, -1
    )
    grad_qkv = contract_rows(normed_first, d_packed)
    d_normed_first = contract_cols(d_packed, qkv_back)
    _, first_pull = jax.vjp(layer_norm, stream, gains_back[0], shifts[0])
    d_stream_first, d_gain_first, d_shift_first = first_pull(d_normed_first)
    d_stream = d_stream_mid + d_stream_first
    per_code = jnp.sum(d_stream.reshape(tokens // RATIO, RATIO, -1), axis=1)
    grad_table = jax.ops.segment_sum(per_code, cond_codes[0], num_segments=VOCAB)
    grad_level = jnp.where(chosen[:, None], jnp.sum(d_stream, axis=0)[None, :], 0.0)
    grad_gain = jnp.stack((d_gain_first, d_gain_second))
    grad_shift = jnp.stack((d_shift_first, d_shift_second))
    reduced = (
        lax.psum_scatter(grad_qkv, ("win", "blk"), scatter_dimension=0, tiled=True),
        lax.psum_scatter(grad_attn, ("win", "blk"), scatter_dimension=1, tiled=True),
        lax.psum_scatter(grad_expand, ("win", "blk"), scatter_dimension=0, tiled=True),
        lax.psum_scatter(grad_reduce, ("win", "blk"), scatter_dimension=0, tiled=True),
        lax.psum_scatter(grad_table, ("win", "blk"), scatter_dimension=0, tiled=True),
        lax.psum_scatter(grad_level, ("win", "blk"), scatter_dimension=1, tiled=True),
        lax.psum_scatter(grad_gain, ("win", "blk"), scatter_dimension=1, tiled=True),
        lax.psum_scatter(grad_shift, ("win", "blk"), scatter_dimension=1, tiled=True),
    )
    return (
        block_out[None],
        d_stream[None],
        reduced[0],
        reduced[1],
        reduced[2],
        reduced[3],
        reduced[4],
        reduced[5],
        reduced[6],
        reduced[7],
    )


def solution(mesh):
    return jax.shard_map(
        body,
        mesh=mesh,
        in_specs=(
            P("win", "blk", None),
            P("win", "blk"),
            P("win"),
            P(("win", "blk"), None),
            P(None, ("win", "blk")),
            P(("win", "blk"), None),
            P(("win", "blk"), None),
            P(("win", "blk"), None),
            P(None, ("win", "blk")),
            P(None, ("win", "blk")),
            P(None, ("win", "blk")),
            P("win", "blk", None),
        ),
        out_specs=(
            P("win", "blk", None),
            P("win", "blk", None),
            P(("win", "blk"), None),
            P(None, ("win", "blk")),
            P(("win", "blk"), None),
            P(("win", "blk"), None),
            P(("win", "blk"), None),
            P(None, ("win", "blk")),
            P(None, ("win", "blk")),
            P(None, ("win", "blk")),
        ),
        check_vma=False,
    )
```

profile of v0, /device:TPU:0, one launch (start us, length us, event | category | flops | bytes accessed | tf_op | source)
XLA Modules:
  0.0 2610.5 jit_solution(1315493941870655193)
XLA Ops:
  10.6 316.7 %all-gather = bf16[128,15,2]{1,2,0:T(2,128)(2,1)S(1)} all-gather(bf16[1,15,2]{1,2,0:T(2,128)(2,1)} %bitcast.154), channel_id=1, replica_groups=mesh['win'=4,'blk'=32] {'win','blk'}, dimensions={0}, use_global_device_ids=true | all-gather | bytes 7740 | tf_op jit(solution)/shard_map/all_gather | solution.py:64
  328.4 342.3 %all-gather.2 = bf16[128,15,2]{1,2,0:T(2,128)(2,1)S(1)} all-gather(bf16[1,15,2]{1,2,0:T(2,128)(2,1)} %bitcast.155), channel_id=1, replica_groups=mesh['win'=4,'blk'=32] {'win','blk'}, dimensions={0}, use_global_device_ids=true | all-gather | bytes 7740 | tf_op jit(solution)/shard_map/all_gather | solution.py:66
  671.1 346.8 %all-gather.1 = bf16[128,15,2]{1,2,0:T(2,128)(2,1)S(1)} all-gather(bf16[1,15,2]{1,2,0:T(2,128)(2,1)} %bitcast.156), channel_id=1, replica_groups=mesh['win'=4,'blk'=32] {'win','blk'}, dimensions={0}, use_global_device_ids=true | all-gather | bytes 7740 | tf_op jit(solution)/shard_map/all_gather | solution.py:65
  1020.0 8.9 reshape.462
  1049.8 44.6 %all-to-all-start = ((bf16[2,128,1440]{2,0,1:T(2,128)(2,1)}), bf16[2,128,1440]{2,0,1:T(2,128)(2,1)S(1)}, u32[]{:S(2)}, u32[]{:S(2)}) async-start(bf16[2,128,1440]{2,0,1:T(2,128)(2,1)} %copy.63), calls=%async_computation | async-start | bytes 1572864 | tf_op jit(solution)/shard_map/all_to_all | solution.py:85
  1094.4 12.5 all-to-all-done
  1120.9 133.1 %all-gather.21.cloned.1.call-done = bf16[128,15,1920]{2,1,0:T(8,128)(2,1)} async-done(((bf16[1,15,1920]{2,1,0:T(8,128)(2,1)}), bf16[128,15,1920]{2,1,0:T(8,128)(2,1)}) %all-gather.21.cloned.1.call-update) | async-done | bytes 7372816 | tf_op jit(solution)/shard_map/all_gather | solution.py:62
  1253.9 9.3 reshape.468
  1263.2 303.3 %all-gather.19.cloned.1.call-done = bf16[128,15,1920]{2,1,0:T(8,128)(2,1)} async-done(((bf16[1,15,1920]{2,1,0:T(8,128)(2,1)}), bf16[128,15,1920]{2,1,0:T(8,128)(2,1)}) %all-gather.19.cloned.1.call-update) | async-done | bytes 7372816 | tf_op jit(solution)/shard_map/all_gather | solution.py:61
  1566.5 9.3 reshape.466
  1598.4 29.0 %all_to_all.60 = bf16[2,128,480]{2,0,1:T(2,128)(2,1)S(1)} all-to-all(bf16[2,128,480]{2,0,1:T(2,128)(2,1)} %copy.71), channel_id=1, replica_groups=mesh['win'=4,'blk'=32] {'blk'}, dimensions={1} | all-to-all | bytes 491520 | tf_op jit(solution)/shard_map/all_to_all | solution.py:132
  1641.1 19.4 all_to_all.61
  1663.9 6.3 multiply_reduce_fusion.1
  1680.1 8.5 scatter_custom_fusion
  1700.0 7.7 fusion.24
  1707.7 7.5 fusion.42
  1721.2 668.9 %fusion.44 = (f32[16,1440]{1,0:T(8,128)S(1)}, f32[480,16]{0,1:T(8,128)S(1)}, f32[16,1920]{1,0:T(8,128)S(1)}, f32[16,1920]{1,0:T(8,128)S(1)}) fusion(f32[1920,1440]{1,0:T(8,128)} %fusion.51, f32[480,1920]{0,1:T(8,128)} %fusion.52, f32[1920,1920]{1,0:T(8,128)} %fusion.42, f32[1920,1920]{1,0:T(8,128)} %fusion.24), kind=kCustom, calls=%all-reduce-scatter.4 | all-reduce-scatter fusion | flops 11796481 | bytes 44605440
  2396.2 7.1 fusion.7
  2441.1 7.5 collective-permute-start.3
  2459.1 7.0 collective-permute-start.23
  2466.1 64.7 %all-reduce.11 = (f32[2,1920]{1,0:T(2,128)S(1)}, f32[2,1920]{1,0:T(2,128)S(1)}, f32[2,1920]{1,0:T(2,128)S(1)}) all-reduce(f32[2,1920]{1,0:T(2,128)S(1)} %broadcast_select_fusion, f32[2,1920]{1,0:T(2,128)S(1)} %pad_maximum_fusion.1, f32[2,1920]{1,0:T(2,128)S(1)} %pad_maximum_fusion.2), channel_id=7, replica_groups=mesh['win'=4,'blk'=32] {'win','blk'}, use_global_device_ids=true, to_apply=%region_20.21.clone | all-reduce | flops 11520 | bytes 92160
  2564.3 8.2 collective-permute-start.30
  2572.6 6.2 collective-permute-start.29
  2585.8 6.2 collective-permute-start.26
  (241 shorter events, 213.0 us)
Async XLA Ops:
  7.2 1012.8 %all-gather.15.cloned.1.call-start = ((), (), s32[]{:S(2)}) async-start(), calls=%async_computation.7 | async-start | bytes 6340608 | tf_op jit(solution)/shard_map/all_gather | solution.py:59
  7.9 1020.9 %all-gather.13.cloned.1.call-start = ((), (), s32[]{:S(2)}) async-start(), calls=%async_computation.5 | async-start | bytes 7925760 | tf_op jit(solution)/shard_map/all_gather | solution.py:63
  8.7 1108.1 %all-gather.17.cloned.1.call-start = ((), (), s32[]{:S(2)}) async-start(), calls=%async_computation.8 | async-start | bytes 2113536 | tf_op jit(solution)/shard_map/all_gather | solution.py:60
  9.4 1244.5 %all-gather.21.cloned.1.call-start = ((), (), s32[]{:S(2)}) async-start(), calls=%async_computation.10 | async-start | bytes 7925760 | tf_op jit(solution)/shard_map/all_gather | solution.py:62
  10.0 1556.6 %all-gather.19.cloned.1.call-start = ((), (), s32[]{:S(2)}) async-start(), calls=%async_computation.9 | async-start | bytes 7925760 | tf_op jit(solution)/shard_map/all_gather | solution.py:61
  1049.8 57.2 %all-to-all-start = ((bf16[2,128,1440]{2,0,1:T(2,128)(2,1)}), bf16[2,128,1440]{2,0,1:T(2,128)(2,1)S(1)}, u32[]{:S(2)}, u32[]{:S(2)}) async-start(bf16[2,128,1440]{2,0,1:T(2,128)(2,1)} %copy.63), calls=%async_computation | async-start | bytes 1572864 | tf_op jit(solution)/shard_map/all_to_all | solution.py:85
  1111.8 464.0 %all-to-all-start.1 = ((bf16[64,4,480]{2,1,0:T(4,128)(2,1)}), bf16[64,4,480]{2,1,0:T(4,128)(2,1)S(1)}, u32[]{:S(2)}, u32[]{:S(2)}) async-start(bf16[64,4,480]{2,1,0:T(4,128)(2,1)} %copy.69), calls=%async_computation.1 | async-start | bytes 524288 | tf_op jit(solution)/shard_map/all_to_all | solution.py:100
  1116.6 1486.5 %reduce-scatter.13.cloned.1.call-start = ((), (), s32[]{:S(2)}) async-start(), calls=%async_computation.6 | async-start | bytes 15851520 | tf_op jit(solution)/shard_map/reduce_scatter | solution.py:175
  2390.1 29.8 %collective-permute-start.14 = (f32[480,16]{0,1:T(8,128)S(1)}, f32[480,16]{0,1:T(8,128)S(1)}, u32[]{:S(2)}, u32[]{:S(2)}) collective-permute-start(f32[480,16]{0,1:T(8,128)S(1)} %get-tuple-element.28), channel_id=1, source_target_pairs={{0,7},{1,8},{2,9},{3,10},{4,11},{5,12},{6,13},{7,14},{8,15},{9,16}... | collective-permute-start | bytes 92168
  2425.0 28.1 %collective-permute-start.6 = (f32[16,1440]{1,0:T(8,128)S(1)}, f32[16,1440]{1,0:T(8,128)S(1)}, u32[]{:S(2)}, u32[]{:S(2)}) collective-permute-start(f32[16,1440]{1,0:T(8,128)S(1)} %get-tuple-element.27), channel_id=1, source_target_pairs={{0,7},{1,8},{2,9},{3,10},{4,11},{5,12},{6,13},{7,14},{8,15},{9,16}... | collective-permute-start | bytes 276488
  2428.2 27.2 %collective-permute-start.5 = (f32[16,1440]{1,0:T(8,128)S(1)}, f32[16,1440]{1,0:T(8,128)S(1)}, u32[]{:S(2)}, u32[]{:S(2)}) collective-permute-start(f32[16,1440]{1,0:T(8,128)S(1)} %get-tuple-element.27), channel_id=1, source_target_pairs={{0,6},{1,7},{2,8},{3,9},{4,10},{5,11},{6,12},{7,13},{8,14},{9,15},... | collective-permute-start | bytes 276488
  2433.2 25.9 collective-permute-start.4
  2441.1 89.8 %collective-permute-start.3 = (f32[16,1440]{1,0:T(8,128)S(1)}, f32[16,1440]{1,0:T(8,128)S(1)}, u32[]{:S(2)}, u32[]{:S(2)}) collective-permute-start(f32[16,1440]{1,0:T(8,128)S(1)} %get-tuple-element.27), channel_id=1, source_target_pairs={{0,4},{1,5},{2,6},{3,7},{4,8},{5,9},{6,10},{7,11},{8,12},{9,13},{1... | collective-permute-start | bytes 276488
  2448.6 85.6 %collective-permute-start.2 = (f32[16,1440]{1,0:T(8,128)S(1)}, f32[16,1440]{1,0:T(8,128)S(1)}, u32[]{:S(2)}, u32[]{:S(2)}) collective-permute-start(f32[16,1440]{1,0:T(8,128)S(1)} %get-tuple-element.27), channel_id=1, source_target_pairs={{0,3},{1,4},{2,5},{3,6},{4,7},{5,8},{6,9},{7,10},{8,11},{9,12},{10... | collective-permute-start | bytes 276488
  2453.1 85.4 %collective-permute-start.1 = (f32[16,1440]{1,0:T(8,128)S(1)}, f32[16,1440]{1,0:T(8,128)S(1)}, u32[]{:S(2)}, u32[]{:S(2)}) collective-permute-start(f32[16,1440]{1,0:T(8,128)S(1)} %get-tuple-element.27), channel_id=1, source_target_pairs={{0,2},{1,3},{2,4},{3,5},{4,6},{5,7},{6,8},{7,9},{8,10},{9,11},{10,... | collective-permute-start | bytes 276488
  2455.4 86.9 %collective-permute-start = (f32[16,1440]{1,0:T(8,128)S(1)}, f32[16,1440]{1,0:T(8,128)S(1)}, u32[]{:S(2)}, u32[]{:S(2)}) collective-permute-start(f32[16,1440]{1,0:T(8,128)S(1)} %get-tuple-element.27), channel_id=1, source_target_pairs={{0,1},{1,2},{2,3},{3,4},{4,5},{5,6},{6,7},{7,8},{8,9},{9,10},{10,1... | collective-permute-start | bytes 276488
  2459.1 87.4 %collective-permute-start.23 = (f32[15,1920]{1,0:T(8,128)S(1)}, f32[15,1920]{1,0:T(8,128)S(1)}, u32[]{:S(2)}, u32[]{:S(2)}) collective-permute-start(f32[15,1920]{1,0:T(8,128)S(1)} %slice.41), channel_id=1, source_target_pairs={{0,8},{1,9},{2,10},{3,11},{4,12},{5,13},{6,14},{7,15},{8,16},{9,17... | collective-permute-start | bytes 345608
  2530.8 28.3 %collective-permute-start.22 = (f32[16,1920]{1,0:T(8,128)S(1)}, f32[16,1920]{1,0:T(8,128)S(1)}, u32[]{:S(2)}, u32[]{:S(2)}) collective-permute-start(f32[16,1920]{1,0:T(8,128)S(1)} %get-tuple-element.29), channel_id=1, source_target_pairs={{0,7},{1,8},{2,9},{3,10},{4,11},{5,12},{6,13},{7,14},{8,15},{9,16}... | collective-permute-start | bytes 368648
  2534.2 27.9 %collective-permute-start.21 = (f32[16,1920]{1,0:T(8,128)S(1)}, f32[16,1920]{1,0:T(8,128)S(1)}, u32[]{:S(2)}, u32[]{:S(2)}) collective-permute-start(f32[16,1920]{1,0:T(8,128)S(1)} %get-tuple-element.29), channel_id=1, source_target_pairs={{0,6},{1,7},{2,8},{3,9},{4,10},{5,11},{6,12},{7,13},{8,14},{9,15},... | collective-permute-start | bytes 368648
  2538.6 25.7 collective-permute-start.20
  2542.3 30.2 %collective-permute-start.19 = (f32[16,1920]{1,0:T(8,128)S(1)}, f32[16,1920]{1,0:T(8,128)S(1)}, u32[]{:S(2)}, u32[]{:S(2)}) collective-permute-start(f32[16,1920]{1,0:T(8,128)S(1)} %get-tuple-element.29), channel_id=1, source_target_pairs={{0,4},{1,5},{2,6},{3,7},{4,8},{5,9},{6,10},{7,11},{8,12},{9,13},{1... | collective-permute-start | bytes 368648
  2553.0 29.3 %collective-permute-start.18 = (f32[16,1920]{1,0:T(8,128)S(1)}, f32[16,1920]{1,0:T(8,128)S(1)}, u32[]{:S(2)}, u32[]{:S(2)}) collective-permute-start(f32[16,1920]{1,0:T(8,128)S(1)} %get-tuple-element.29), channel_id=1, source_target_pairs={{0,3},{1,4},{2,5},{3,6},{4,7},{5,8},{6,9},{7,10},{8,11},{9,12},{10... | collective-permute-start | bytes 368648
  2559.1 24.5 collective-permute-start.17
  2564.3 27.8 %collective-permute-start.30 = (f32[16,1920]{1,0:T(8,128)S(1)}, f32[16,1920]{1,0:T(8,128)S(1)}, u32[]{:S(2)}, u32[]{:S(2)}) collective-permute-start(f32[16,1920]{1,0:T(8,128)S(1)} %get-tuple-element.30), channel_id=1, source_target_pairs={{0,7},{1,8},{2,9},{3,10},{4,11},{5,12},{6,13},{7,14},{8,15},{9,16}... | collective-permute-start | bytes 368648
  (47 other events, 426.3 us)
Sparse Core Ops, SparseCore 0:
  9.7 313.0 all-gather.14
  324.4 313.8 all-gather.12
  640.0 299.8 all-gather.16
  941.4 312.4 all-gather.20
  1255.5 311.0 all-gather.18
  1688.8 752.4 reduce-scatter.12
where the time goes:
time: 2630 us; the launch traced here: 2610 us
  blocking collectives  1790 us (68%)
  waiting for transfers between devices  455 us (17%)
  starting transfers between devices  178 us (7%)
  local copies, waits for them, and re-layouts  90.3 us (3%)
  matrix products  60.1 us (2%)
    unnamed x2, blocking collectives  734 us
    all_gather x1, blocking collectives, body(): lax.all_gather(norm_gain, ('win', 'blk'), axis=1, tiled=True)  347 us
    all_gather x1, blocking collectives, body(): lax.all_gather(norm_bias, ('win', 'blk'), axis=1, tiled=True)  342 us
    all_gather x1, blocking collectives, body(): lax.all_gather(level_table, ('win', 'blk'), axis=1, tiled=True)  317 us
    all_gather x1, waiting for transfers between devices, body(): lax.all_gather(mlp_in_weight, ('win', 'blk'), axis=0, tiled=True)  303 us
    all_gather x1, waiting for transfers between devices, body(): lax.all_gather(mlp_out_weight, ('win', 'blk'), axis=0, tiled=True)  133 us
    unnamed x32, starting transfers between devices  129 us
  transfers between devices with their start and end apart: 40, of which 5 were waited for; matrix products, arithmetic and copies ran while one was open for 30% of the time, Pallas kernels for 0%

commit v1 on v0

v1 whole, which is shorter than its diff:
```python
import jax
import jax.numpy as jnp
from jax import lax
from jax.sharding import Mesh, PartitionSpec as P

HEAD = 480
BLOCK = 128
RATIO = 4
D = 1920
SHARDS = 128
ROWS = 16
PART = 640
epsilon = 1e-05
bf16 = jnp.bfloat16
f32 = jnp.float32
AXES = ("yl", "co", "yh", "z", "x")
WIN = ("yl", "co")
BLK = ("yh", "z", "x")
STEP_BITS = {"x": (1, 3), "z": (4, 12), "y": (64, 80)}
CORE_BIT = 32
ORDERS = (("x", "z", "y"), ("z", "y", "x"), ("y", "x", "z"))
RANK = {"y": 0, "z": 1, "x": 2}


def exchange(value, axis, step):
    pairs = []
    for device in range(SHARDS):
        core = (device >> 5) & 1
        pairs.append((device, device ^ STEP_BITS[axis][step ^ core]))
    return lax.ppermute(value, AXES, pairs)


def swap_cores(value):
    return lax.ppermute(value, AXES, [(i, i ^ CORE_BIT) for i in range(SHARDS)])


def bit_place(done, axis, step):
    return sum(1 for other in done if (RANK[other[0]], -other[1]) < (RANK[axis], -step))


def gather_steps(buf, order, done, steps):
    for axis, step in steps:
        place = bit_place(done, axis, step)
        buf = jnp.stack((buf, exchange(buf, axis, step)), axis=place)
        done = done + ((axis, step),)
    return buf, done


def all_steps(order):
    return [(axis, step) for axis in order for step in (0, 1)]


def scatter_steps(buf, done, steps):
    for axis, step in steps:
        done = tuple(d for d in done if d != (axis, step))
        place = bit_place(done, axis, step)
        kept = lax.index_in_dim(buf, 0, place, keepdims=False)
        sent = lax.index_in_dim(buf, 1, place, keepdims=False)
        got = exchange(sent, axis, step)
        buf = (kept.astype(f32) + got.astype(f32)).astype(bf16)
    return buf, done


def layer_norm(stream, gain, shift):
    average = jnp.mean(stream, axis=-1, keepdims=True)
    centered = stream - average
    variance = jnp.mean(centered * centered, axis=-1, keepdims=True)
    return centered * lax.rsqrt(variance + epsilon) * gain + shift


def rows_dot(left, right):
    return lax.dot_general(left, right, (((0,), (0,)), ((), ())), preferred_element_type=f32)


def cols_dot(left, right):
    return lax.dot_general(left, right, (((1,), (1,)), ((), ())), preferred_element_type=f32)


def dot(left, right):
    return jnp.dot(left, right, preferred_element_type=f32)


def attention_mask():
    row = jnp.arange(256)
    block = (row // 8) * 2 + (row // 4) % 2
    column = row % 4
    return (column[:, None] == column[None, :]) & (block[:, None] >= block[None, :])


def rel_shards(yl, co, yh, z, x, core):
    place = jnp.arange(64)
    first = jnp.where(core == 0, 1, 3)
    second = jnp.where(core == 0, 3, 1)

    def offset(high, low):
        return ((place >> low) & 1) * first ^ ((place >> high) & 1) * second

    along_y = offset(5, 4) ^ (yh * 2 + yl)
    along_z = offset(3, 2) ^ z
    along_x = offset(1, 0) ^ x
    return (along_y & 1) * 64 + core * 32 + (along_y >> 1) * 16 + along_z * 4 + along_x


def body(
    hidden_in,
    cond_codes,
    level_ids,
    qkv_weight,
    attn_out_weight,
    mlp_in_weight,
    mlp_out_weight,
    code_table,
    level_table,
    norm_gain,
    norm_bias,
    grad_out,
):
    yl, co, yh, z, x = (lax.axis_index(name) for name in AXES)
    vectors = jnp.concatenate((norm_gain, norm_bias, level_table), axis=0).reshape(1, 90)
    shard0 = jnp.concatenate(
        (
            jnp.concatenate((qkv_weight, attn_out_weight.T), axis=1),
            jnp.pad(vectors, ((0, 0), (0, D - 90))),
        ),
        axis=0,
    )
    shard1 = jnp.pad(mlp_in_weight, ((0, 1), (0, 0)))
    shard2 = jnp.pad(mlp_out_weight, ((0, 1), (0, 0)))
    shards = (shard0, code_table, shard1, shard2)
    early, late = [], []
    for part, order in enumerate(ORDERS):
        cut = slice(part * PART, (part + 1) * PART)
        buf = jnp.concatenate([s[:, cut] for s in shards], axis=1)
        steps = all_steps(order)
        buf, done = gather_steps(buf, order, (), steps[:4])
        first, _ = gather_steps(buf[..., : 2 * PART], order, done, steps[4:])
        second, _ = gather_steps(buf[..., 2 * PART :], order, done, steps[4:])
        early.append(first)
        late.append(second)

    def assemble(bufs, index):
        cut = slice(index * PART, (index + 1) * PART)
        own = jnp.concatenate([b[0][..., cut].reshape(1024, PART) for b in bufs], axis=1)
        other = jnp.concatenate([b[1][..., cut].reshape(1024, PART) for b in bufs], axis=1)
        return jnp.concatenate((own, other), axis=0)

    early = [(b, swap_cores(b)) for b in early]
    late = [(b, swap_cores(b)) for b in late]
    full0, table = assemble(early, 0), assemble(early, 1)
    expand, reduce = assemble(late, 0), assemble(late, 1)

    shard_of = jnp.concatenate(
        (rel_shards(yl, co, yh, z, x, co), rel_shards(yl, co, yh, z, x, 1 - co))
    )
    feature = jnp.arange(D)
    place_feature = (shard_of[:, None] * 15 + jnp.arange(ROWS)[None, :]).reshape(-1)
    place_feature = jnp.where(jnp.arange(SHARDS * ROWS) % ROWS < 15, place_feature, -1)
    shuffle = (feature[:, None] == place_feature[None, :]).astype(bf16)
    shard_hot = (shard_of[:, None] == feature[None, :] // 15).astype(bf16)
    vector_mask = (jnp.arange(90)[:, None] % 15) == (feature[None, :] % 15)
    place_code = (shard_of[:, None] * 16 + jnp.arange(ROWS)[None, :]).reshape(-1)
    codes = jnp.repeat(cond_codes[0], RATIO)
    code_hot = (codes[:, None] == place_code[None, :]).astype(bf16)

    small = full0.reshape(SHARDS, ROWS, D)[:, 15, :90]
    spread = jnp.where(vector_mask, rows_dot(small, shard_hot), 0.0)
    spread = jnp.sum(spread.reshape(6, 15, D), axis=1)
    gains, shifts, levels = spread[0:2], spread[2:4], spread[4:6]
    chosen = jnp.arange(2) == level_ids[0]
    level_row = jnp.sum(jnp.where(chosen[:, None], levels, 0.0), axis=0)

    hidden = hidden_in[0].astype(f32)
    stream = hidden + dot(code_hot, table) + level_row[None, :]
    normed_first = layer_norm(stream, gains[0], shifts[0]).astype(bf16)
    first_shuffled = dot(normed_first, shuffle).astype(bf16)
    packed = dot(first_shuffled, full0[:, :1440]).astype(bf16)

    token = jnp.arange(256)
    moved = (token // 4 % 2) * 128 + (token // 8) * 4 + token % 4
    row_move = (moved[:, None] == token[None, :]).astype(bf16)

    def to_columns(value):
        value = dot(row_move, value).astype(bf16)
        return lax.all_to_all(value, BLK, split_axis=0, concat_axis=0, tiled=True)

    def to_tokens(value):
        value = lax.all_to_all(value, BLK, split_axis=0, concat_axis=0, tiled=True)
        return rows_dot(row_move, value).astype(bf16)

    columns = to_columns(packed)
    query, key, value = columns[:, :480], columns[:, 480:960], columns[:, 960:]
    mask = attention_mask()

    scores = jnp.where(mask, cols_dot(query, key) * HEAD ** (-0.5), -1e30)
    row_top = jnp.max(scores, axis=-1, keepdims=True)
    log_total = row_top + jnp.log(jnp.sum(jnp.exp(scores - row_top), axis=-1, keepdims=True))
    probs = jnp.exp(scores - log_total)
    probs_low = probs.astype(bf16)
    mixed = to_tokens(dot(probs_low, value).astype(bf16))

    attn_rows = dot(shuffle, full0[:, 1440:]).astype(bf16)
    stream_mid = stream + cols_dot(mixed, attn_rows)
    normed_second = layer_norm(stream_mid, gains[1], shifts[1]).astype(bf16)
    second_shuffled = dot(normed_second, shuffle).astype(bf16)
    upward = dot(second_shuffled, expand)
    active, gelu_pull = jax.vjp(lambda pre: jax.nn.gelu(pre, approximate=True), upward)
    active = active.astype(bf16)
    active_shuffled = dot(active, shuffle).astype(bf16)
    block_out = (stream_mid + dot(active_shuffled, reduce)).astype(bf16)

    upstream = grad_out[0]
    grad_reduce = rows_dot(active_shuffled, upstream).astype(bf16)
    d_active = cols_dot(cols_dot(upstream, reduce).astype(bf16), shuffle)
    d_upward = gelu_pull(d_active)[0].astype(bf16)
    grad_expand = rows_dot(second_shuffled, d_upward).astype(bf16)
    d_second = cols_dot(cols_dot(d_upward, expand).astype(bf16), shuffle)
    _, second_pull = jax.vjp(layer_norm, stream_mid, gains[1], shifts[1])
    d_mid_part, d_gain_second, d_shift_second = second_pull(d_second)
    d_stream_mid = upstream.astype(f32) + d_mid_part
    d_attn = d_stream_mid.astype(bf16)
    attn_shuffled = dot(d_attn, shuffle).astype(bf16)
    grad_attn = rows_dot(attn_shuffled, mixed).astype(bf16)
    d_mixed = to_columns(dot(d_attn, attn_rows).astype(bf16))

    def scatter_parts(arrays, count):
        bufs = []
        for part, order in enumerate(ORDERS):
            cut = slice(part * PART, (part + 1) * PART)
            kept = jnp.concatenate([a[:1024, cut] for a in arrays], axis=1)
            sent = jnp.concatenate([a[1024:, cut] for a in arrays], axis=1)
            buf = (kept.astype(f32) + swap_cores(sent).astype(f32)).astype(bf16)
            buf = buf.reshape(2, 2, 2, 2, 2, 2, ROWS, len(arrays) * PART)
            steps = all_steps(order)
            buf, done = scatter_steps(buf, tuple(steps), steps[::-1][:count])
            bufs.append((buf, done, steps[::-1][count:]))
        return bufs

    sums_early = scatter_parts((grad_expand, grad_reduce), 2)

    d_values = rows_dot(probs_low, d_mixed)
    d_probs = cols_dot(d_mixed, value)
    d_scores = (
        probs * (d_probs - jnp.sum(probs * d_probs, axis=-1, keepdims=True))
    ).astype(bf16)
    d_queries = dot(d_scores, key) * HEAD ** (-0.5)
    d_keys = rows_dot(d_scores, query) * HEAD ** (-0.5)
    d_packed = to_tokens(jnp.concatenate((d_queries, d_keys, d_values), axis=1).astype(bf16))

    grad_qkv = rows_dot(first_shuffled, d_packed).astype(bf16)
    d_first = cols_dot(cols_dot(d_packed, full0[:, :1440]).astype(bf16), shuffle)
    _, first_pull = jax.vjp(layer_norm, stream, gains[0], shifts[0])
    d_stream_part, d_gain_first, d_shift_first = first_pull(d_first)
    d_stream = d_stream_mid + d_stream_part
    grad_table = rows_dot(code_hot, d_stream.astype(bf16)).astype(bf16)

    d_level = jnp.where(chosen[:, None], jnp.sum(d_stream, axis=0)[None, :], 0.0)
    totals = jnp.concatenate(
        (
            jnp.stack((d_gain_first, d_gain_second, d_shift_first, d_shift_second)),
            d_level,
        ),
        axis=0,
    )
    totals = jnp.where(vector_mask, jnp.repeat(totals, 15, axis=0), 0.0).astype(bf16)
    small = cols_dot(shard_hot, totals).astype(bf16)
    small = jnp.pad(small[:, None, :], ((0, 0), (15, 0), (0, D - 90)))
    grad0 = jnp.concatenate((grad_qkv, grad_attn), axis=1) + small.reshape(SHARDS * ROWS, D)

    sums_late = scatter_parts((grad0, grad_table), 2)
    ends = []
    for (a, done, steps), (b, _, _) in zip(sums_late, sums_early):
        buf, _ = scatter_steps(jnp.concatenate((a, b), axis=-1), done, steps)
        ends.append(buf.astype(f32))
    out0, out3, out1, out2 = (
        jnp.concatenate([e[:, i * PART : (i + 1) * PART] for e in ends], axis=1) for i in range(4)
    )
    small = out0[15, :90].reshape(6, 15)
    return (
        block_out[None],
        d_stream[None],
        out0[:15, :1440],
        out0[:15, 1440:].T,
        out1[:15],
        out2[:15],
        out3,
        small[4:6],
        small[0:2],
        small[2:4],
    )


def solution(mesh):
    fine = Mesh(mesh.devices.reshape(2, 2, 2, 4, 4), AXES)
    return jax.shard_map(
        body,
        mesh=fine,
        in_specs=(
            P(WIN, BLK, None),
            P(WIN, BLK),
            P(WIN),
            P(AXES, None),
            P(None, AXES),
            P(AXES, None),
            P(AXES, None),
            P(AXES, None),
            P(None, AXES),
            P(None, AXES),
            P(None, AXES),
            P(WIN, BLK, None),
        ),
        out_specs=(
            P(WIN, BLK, None),
            P(WIN, BLK, None),
            P(AXES, None),
            P(None, AXES),
            P(AXES, None),
            P(AXES, None),
            P(AXES, None),
            P(None, AXES),
            P(None, AXES),
            P(None, AXES),
        ),
        check_vma=False,
    )
```

time: 2630 us -> 649 us (0.25)
  blocking collectives: 1790 us -> 0 us
  waiting for transfers between devices: 455 us -> 96.1 us
  other arithmetic: 23.1 us -> 170 us
  matrix products: 60.1 us -> 127 us
  starting transfers between devices: 178 us -> 120 us
  local copies, waits for them, and re-layouts: 90.3 us -> 120 us
    all_gather x3 -> x0, blocking collectives: 1010 us -> none  [the longest x1 347 us: body(): lax.all_gather(norm_gain, ('win', 'blk'), axis=1, tiled=True)]
    unnamed x2 -> x0, blocking collectives: 734 us -> none
    all_gather x5 -> x0, waiting for transfers between devices: 436 us -> none  [the longest x1 303 us: body(): lax.all_gather(mlp_in_weight, ('win', 'blk'), axis=0, tiled=True)]
    unnamed x32 -> x0, starting transfers between devices: 129 us -> none
    concatenate x0 -> x14, other arithmetic: none -> 103 us  [the longest x2 86.2 us: assemble(): return jnp.concatenate((own, other), axis=0)]
    ppermute x0 -> x60, waiting for transfers between devices: none -> 90.2 us  [the longest x48 90.2 us: exchange(): return lax.ppermute(value, AXES, pairs)]
    ppermute x0 -> x60, starting transfers between devices: none -> 82.4 us  [the longest x48 79.9 us: exchange(): return lax.ppermute(value, AXES, pairs)]
    dot_general x18 -> x28, matrix products: 60.1 us -> 127 us  [the longest x7 46.2 us: cols_dot(): lax.dot_general(left, right, (((1,), (1,)), ((), ())), preferred_element_...]
  transfers between devices with their start and end apart: 40 -> 64, of which waited for: 5 -> 24; matrix products, arithmetic and copies ran while one was open for 30% -> 51% of each run, Pallas kernels for 0% -> 0%
where the time goes in v1:
time: 649 us; the launch traced here: 637 us
  other arithmetic  170 us (26%)
  matrix products  127 us (20%)
  local copies, waits for them, and re-layouts  120 us (18%)
  starting transfers between devices  120 us (18%)
  waiting for transfers between devices  96.1 us (15%)
    ppermute x48, waiting for transfers between devices, exchange(): return lax.ppermute(value, AXES, pairs)  90.2 us
    concatenate x2, other arithmetic, assemble(): return jnp.concatenate((own, other), axis=0)  86.2 us
    ppermute x48, starting transfers between devices, exchange(): return lax.ppermute(value, AXES, pairs)  79.9 us
    dot_general x7, matrix products, cols_dot(): lax.dot_general(left, right, (((1,), (1,)), ((), ())), preferred_element_...  46.2 us
    dot_general x11, matrix products, dot(): return jnp.dot(left, right, preferred_element_type=f32)  45.3 us
    dot_general x10, matrix products, rows_dot(): lax.dot_general(left, right, (((0,), (0,)), ((), ())), preferred_element_...  35.7 us
    convert_element_type x6, other arithmetic, scatter_parts(): buf = (kept.astype(f32) + swap_cores(sent).astype(f32)).astype(bf16)  25.7 us
    all_to_all x2, starting transfers between devices, to_tokens(): value = lax.all_to_all(value, BLK, split_axis=0, concat_axis=0, tiled=True)  20.3 us
  transfers between devices with their start and end apart: 64, of which 24 were waited for; matrix products, arithmetic and copies ran while one was open for 51% of the time, Pallas kernels for 0%

profile of v1, /device:TPU:0, one launch (start us, length us, event | category | flops | bytes accessed | tf_op | source)
XLA Modules:
  0.0 637.1 jit_solution(17361567160979316819)
XLA Ops:
  40.2 6.8 %collective-permute-done.15 = bf16[2,2,2,16,2560]{4,3,1,0,2:T(8,128)(2,1)S(1)} collective-permute-done((bf16[2,2,2,16,2560]{4,3,1,0,2:T(8,128)(2,1)}, bf16[2,2,2,16,2560]{4,3,1,0,2:T(8,128)(2,1)S(1)}, u32[]{:S(2)}, u32[]{:S(2)}) %collective-permute-start.15) | collective-permute-done | bytes 655392 | tf_op jit(solution)/shard_map/ppermute | solution.py:30
  58.3 8.0 %collective-permute-done.16 = bf16[2,2,2,2,16,1280]{5,4,1,0,3,2:T(8,128)(2,1)S(1)} collective-permute-done((bf16[2,2,2,2,16,1280]{5,4,1,0,3,2:T(8,128)(2,1)S(1)}, bf16[2,2,2,2,16,1280]{5,4,1,0,3,2:T(8,128)(2,1)S(1)}, u32[]{:S(2)}, u32[]{:S(2)}) %collective-permute-start.16) | collective-permute-done | bytes 655392 | tf_op jit(solution)/shard_map/ppermute | solution.py:30
  66.3 7.2 %collective-permute-start.26 = (bf16[2,2,2,2,2,16,1280]{6,5,1,0,4,3,2:T(8,128)(2,1)S(1)}, bf16[2,2,2,2,2,16,1280]{6,5,1,0,4,3,2:T(8,128)(2,1)S(1)}, u32[]{:S(2)}, u32[]{:S(2)}) collective-permute-start(bf16[2,2,2,2,2,16,1280]{6,5,1,0,4,3,2:T(8,128)(2,1)S(1)} %get-tuple-element.100), channel_id=1, source_target_pairs={{0,12},{1,13},{2,14},{3,15},{4,8},{5,9},{6,10},{7,11},{8,4},{9,5},... | collective-permute-start | bytes 3932168 | tf_op jit(solution)/shard_map/ppermute | solution.py:30
  89.3 13.8 %collective-permute-done.17 = bf16[2,2,2,2,2,16,1280]{6,5,1,0,4,3,2:T(8,128)(2,1)S(1)} collective-permute-done((bf16[2,2,2,2,2,16,1280]{6,5,1,0,4,3,2:T(8,128)(2,1)S(1)}, bf16[2,2,2,2,2,16,1280]{6,5,1,0,4,3,2:T(8,128)(2,1)S(1)}, u32[]{:S(2)}, u32[]{:S(2)}) %collective-permute-start.17) | collective-permute-done | bytes 1310752 | tf_op jit(solution)/shard_map/ppermute | solution.py:30
  133.7 47.4 %maximum_maximum_fusion = bf16[2048,1920]{1,0:T(8,128)(2,1)S(1)} fusion(bf16[1024,640]{1,0:T(8,128)(2,1)S(1)} %bitcast.378, bf16[1024,640]{1,0:T(8,128)(2,1)S(1)} %bitcast.371, bf16[1024,640]{1,0:T(8,128)(2,1)S(1)} %bitcast.370, bf16[1024,640]{1,0:T(8,128)(2,1)S(1)} %bitcast.377, bf16[1024,640]{1,0:T(8,128)(2,1)S(1)} %bitcast.368, ...), kind=kLoop, calls=%fused_computation.21 | loop fusion | flops 47185920 | bytes 15728640 | tf_op jit(solution)/shard_map/concatenate | solution.py:145
  200.6 6.1 convolution_convert_fusion.8
  209.0 7.4 %all-to-all-start = ((bf16[32,8,1440]{2,1,0:T(8,128)(2,1)}), bf16[32,8,1440]{2,1,0:T(8,128)(2,1)}, u32[]{:S(2)}, u32[]{:S(2)}) async-start(bf16[32,8,1440]{2,1,0:T(8,128)(2,1)} %bitcast.379), calls=%async_computation | async-start | bytes 1572864 | tf_op jit(solution)/shard_map/all_to_all | solution.py:184
  220.0 38.8 %maximum_maximum_fusion.1 = bf16[2048,1920]{1,0:T(8,128)(2,1)} fusion(bf16[1024,640]{1,0:T(8,128)(2,1)} %bitcast.376, bf16[1024,640]{1,0:T(8,128)(2,1)S(1)} %bitcast.375, bf16[1024,640]{1,0:T(8,128)(2,1)S(1)} %bitcast.372, bf16[1024,640]{1,0:T(8,128)(2,1)S(1)} %bitcast.373, bf16[1024,640]{1,0:T(8,128)(2,1)S(1)} %bitcast.374, bf16[1024,640]{1,0:T(8,128)(2,1)S(1)} %bitcast.367), kind=kLoop, calls=%fused_computation.22 | loop fusion | flops 47185920 | bytes 15728640 | tf_op jit(solution)/shard_map/concatenate | solution.py:145
  267.0 10.5 %all-to-all-start.1 = ((bf16[32,8,480]{2,1,0:T(8,128)(2,1)}), bf16[32,8,480]{2,1,0:T(8,128)(2,1)}, u32[]{:S(2)}, u32[]{:S(2)}) async-start(bf16[32,8,480]{2,1,0:T(8,128)(2,1)} %bitcast.407), calls=%async_computation.1 | async-start | bytes 524288 | tf_op jit(solution)/shard_map/all_to_all | solution.py:187
  277.5 8.6 %fusion.32 = bf16[1920,480]{0,1:T(8,128)(2,1)} fusion(s32[2048]{0:T(1024)} %copy-done.59, bf16[2048,1920]{1,0:T(8,128)(2,1)} %copy-done.7), kind=kOutput, calls=%fused_computation.80 | convolution fusion | flops 3779727360 | bytes 3948544 | tf_op jit(solution)/shard_map/dot_general | solution.py:80
  305.2 19.1 %fusion.64 = bf16[256,1920]{1,0:T(8,128)(2,1)} fusion(f32[256,1920]{1,0:T(8,128)} %copy-done.75, s32[2048]{0:T(1024)S(1)} %copy-done.60, bf16[1,256,1920]{2,1,0:T(8,128)(2,1)S(1)} %copy-done.6, bf16[1024,640]{1,0:T(8,128)(2,1)} %bitcast.404, bf16[1024,640]{1,0:T(8,128)(2,1)} %bitcast.402, bf16[1024,640]{1,0:T(8,128)(2,1)} %bitcast.390, ...), kind=kOutput, calls=%fused_computation.125 | convolution fusion | flops 4088004608 | bytes 11804672 | tf_op jit(solution)/shard_map/dot_general | solution.py:76
  324.3 11.1 %multiply_reduce_fusion = (bf16[1920]{0:T(1024)(128)(2,1)S(1)}, f32[256]{0:T(256)S(1)}, bf16[1920]{0:T(1024)(128)(2,1)S(1)}, f32[256,1920]{1,0:T(8,128)}) fusion(f32[256,1920]{1,0:T(8,128)} %copy-done.2, f32[256]{0:T(256)S(1)} %fusion.200, f32[256]{0:T(256)S(1)} %broadcast_multiply_fusion, f32[1920]{0:T(1024)S(1)} %copy-done.42, s32[2048]{0:T(1024)S(1)} %copy-done.60, ...), kind=kOutput, calls=%fused_computation.126 | convolution fusion | flops 4034916352 | bytes 12806144 | tf_op jit(solution)/shard_map/dot_general | solution.py:76
  335.5 7.0 %convolution_convert_fusion.2 = bf16[2048,1920]{0,1:T(8,128)(2,1)} fusion(bf16[256,2048]{1,0:T(8,128)(2,1)} %copy-done.28, bf16[256,1920]{1,0:T(8,128)(2,1)} %fusion.64), kind=kOutput, calls=%fused_computation.35 | convolution fusion | flops 2017198080 | bytes 9895936 | tf_op jit(solution)/shard_map/dot_general | solution.py:72
  358.5 10.1 %all-to-all-start.2 = ((bf16[32,8,480]{2,1,0:T(8,128)(2,1)}), bf16[32,8,480]{2,1,0:T(8,128)(2,1)}, u32[]{:S(2)}, u32[]{:S(2)}) async-start(bf16[32,8,480]{2,1,0:T(8,128)(2,1)} %bitcast.86), calls=%async_computation.2 | async-start | bytes 524288 | tf_op jit(solution)/shard_map/all_to_all | solution.py:184
  396.0 9.9 %all-to-all-start.3 = ((bf16[32,8,1440]{2,1,0:T(8,128)(2,1)}), bf16[32,8,1440]{2,1,0:T(8,128)(2,1)}, u32[]{:S(2)}, u32[]{:S(2)}) async-start(bf16[32,8,1440]{2,1,0:T(8,128)(2,1)} %concatenate.158), calls=%async_computation.3 | async-start | bytes 1572864 | tf_op jit(solution)/shard_map/all_to_all | solution.py:187
  409.5 6.1 convolution_convert_fusion.4
  415.6 5.9 all-to-all-done.3
  424.1 9.6 %multiply_reduce_fusion.1 = (bf16[1920]{0:T(1024)(128)(2,1)S(1)}, f32[256]{0:T(256)S(1)}, bf16[1920]{0:T(1024)(128)(2,1)S(1)}, f32[256,1920]{1,0:T(8,128)}) fusion(f32[256,1920]{1,0:T(8,128)S(1)} %get-tuple-element.158, f32[256]{0:T(256)S(1)} %copy-done.64, f32[256]{0:T(256)S(1)} %copy-done.50, f32[1920]{0:T(1024)S(1)} %copy-done.41, ...), kind=kOutput, calls=%fused_computation.127 | convolution fusion | flops 3531599872 | bytes 10987520 | tf_op jit(solution)/shard_map/dot_general | solution.py:76
  433.7 5.8 convolution_convert_fusion
  446.5 10.8 %copy.65 = bf16[2048,1920]{0,1:T(8,128)(2,1)} copy(bf16[2048,1920]{1,0:T(8,128)(2,1)} %bitcast.344) | data formatting | bytes 15728640 | tf_op jit(solution)/shard_map/reshape | solution.py:267
  457.3 7.0 %maximum_add_fusion = bf16[2048,1920]{0,1:T(8,128)(2,1)S(1)} fusion(bf16[2048,1920]{0,1:T(8,128)(2,1)} %copy.65, bf16[2048,480]{0,1:T(8,128)(2,1)} %convolution_convert_fusion.4, bf16[2048,1440]{0,1:T(8,128)(2,1)} %convolution_convert_fusion), kind=kLoop, calls=%fused_computation.24 | loop fusion | flops 23592960 | bytes 23592960 | tf_op jit(solution)/shard_map/add | solution.py:267
  562.5 5.7 collective-permute-done.35
  571.5 7.5 %collective-permute-done.55 = bf16[2,2,2,2,16,1280]{5,4,1,0,3,2:T(8,128)(2,1)S(1)} collective-permute-done((bf16[2,2,2,2,16,1280]{5,4,1,0,3,2:T(8,128)(2,1)S(1)}, bf16[2,2,2,2,16,1280]{5,4,1,0,3,2:T(8,128)(2,1)S(1)}, u32[]{:S(2)}, u32[]{:S(2)}) %collective-permute-start.55) | collective-permute-done | bytes 655392 | tf_op jit(solution)/shard_map/ppermute | solution.py:30
  584.7 7.0 %collective-permute-done.32 = bf16[2,2,2,2,16,1280]{5,4,3,2,1,0:T(8,128)(2,1)S(1)} collective-permute-done((bf16[2,2,2,2,16,1280]{5,4,3,2,1,0:T(8,128)(2,1)S(1)}, bf16[2,2,2,2,16,1280]{5,4,3,2,1,0:T(8,128)(2,1)S(1)}, u32[]{:S(2)}, u32[]{:S(2)}) %collective-permute-start.32) | collective-permute-done | bytes 655392 | tf_op jit(solution)/shard_map/ppermute | solution.py:30
  (493 shorter events, 356.6 us)
Async XLA Ops:
  51.6 25.7 %collective-permute-start.21 = (bf16[2,2,2,2,16,1280]{5,4,3,2,1,0:T(8,128)(2,1)S(1)}, bf16[2,2,2,2,16,1280]{5,4,3,2,1,0:T(8,128)(2,1)S(1)}, u32[]{:S(2)}, u32[]{:S(2)}) collective-permute-start(bf16[2,2,2,2,16,1280]{5,4,3,2,1,0:T(8,128)(2,1)S(1)} %get-tuple-element.93), channel_id=1, source_target_pairs={{0,64},{1,65},{2,66},{3,67},{4,68},{5,69},{6,70},{7,71},{8,72},{9,... | collective-permute-start | bytes 1966088 | tf_op jit(solution)/shard_map/ppermute | solution.py:30
  53.7 23.9 %collective-permute-start.10 = (bf16[2,2,2,2,16,1280]{5,4,3,2,1,0:T(8,128)(2,1)S(1)}, bf16[2,2,2,2,16,1280]{5,4,3,2,1,0:T(8,128)(2,1)S(1)}, u32[]{:S(2)}, u32[]{:S(2)}) collective-permute-start(bf16[2,2,2,2,16,1280]{5,4,3,2,1,0:T(8,128)(2,1)S(1)} %get-tuple-element.98), channel_id=1, source_target_pairs={{0,1},{1,0},{2,3},{3,2},{4,5},{5,4},{6,7},{7,6},{8,9},{9,8},{10,11... | collective-permute-start | bytes 1966088 | tf_op jit(solution)/shard_map/ppermute | solution.py:30
  73.7 29.4 %collective-permute-start.17 = (bf16[2,2,2,2,2,16,1280]{6,5,1,0,4,3,2:T(8,128)(2,1)S(1)}, bf16[2,2,2,2,2,16,1280]{6,5,1,0,4,3,2:T(8,128)(2,1)S(1)}, u32[]{:S(2)}, u32[]{:S(2)}) collective-permute-start(bf16[2,2,2,2,2,16,1280]{6,5,1,0,4,3,2:T(8,128)(2,1)S(1)} %get-tuple-element.108), channel_id=1, source_target_pairs={{0,12},{1,13},{2,14},{3,15},{4,8},{5,9},{6,10},{7,11},{8,4},{9,5},... | collective-permute-start | bytes 3932168 | tf_op jit(solution)/shard_map/ppermute | solution.py:30
  77.3 26.1 %collective-permute-start.5 = (bf16[2,2,2,2,2,16,1280]{6,5,4,3,2,1,0:T(8,128)(2,1)S(1)}, bf16[2,2,2,2,2,16,1280]{6,5,4,3,2,1,0:T(8,128)(2,1)S(1)}, u32[]{:S(2)}, u32[]{:S(2)}) collective-permute-start(bf16[2,2,2,2,2,16,1280]{6,5,4,3,2,1,0:T(8,128)(2,1)S(1)} %get-tuple-element.104), channel_id=1, source_target_pairs={{0,80},{1,81},{2,82},{3,83},{4,84},{5,85},{6,86},{7,87},{8,88},{9,... | collective-permute-start | bytes 3932168 | tf_op jit(solution)/shard_map/ppermute | solution.py:30
  77.6 32.7 %collective-permute-start.22 = (bf16[2,2,2,2,2,16,1280]{6,5,4,3,2,1,0:T(8,128)(2,1)S(1)}, bf16[2,2,2,2,2,16,1280]{6,5,4,3,2,1,0:T(8,128)(2,1)S(1)}, u32[]{:S(2)}, u32[]{:S(2)}) collective-permute-start(bf16[2,2,2,2,2,16,1280]{6,5,4,3,2,1,0:T(8,128)(2,1)S(1)} %get-tuple-element.92), channel_id=1, source_target_pairs={{0,80},{1,81},{2,82},{3,83},{4,84},{5,85},{6,86},{7,87},{8,88},{9,... | collective-permute-start | bytes 3932168 | tf_op jit(solution)/shard_map/ppermute | solution.py:30
  89.1 35.0 %collective-permute-start.28 = (bf16[2,2,2,2,2,2,16,1280]{7,6,3,2,1,0,5,4:T(8,128)(2,1)S(1)}, bf16[2,2,2,2,2,2,16,1280]{7,6,3,2,1,0,5,4:T(8,128)(2,1)S(1)}, u32[]{:S(2)}, u32[]{:S(2)}) collective-permute-start(bf16[2,2,2,2,2,2,16,1280]{7,6,3,2,1,0,5,4:T(8,128)(2,1)S(1)} %pad_maximum_fusion.4), channel_id=1, source_target_pairs={{0,32},{1,33},{2,34},{3,35},{4,36},{5,37},{6,38},{7,39},{8,40},{9,... | collective-permute-start | bytes 7864328 | tf_op jit(solution)/shard_map/ppermute | solution.py:34
  103.4 25.4 %collective-permute-start.20 = (bf16[2,2,2,2,2,2,16,1280]{7,6,1,0,5,4,3,2:T(8,128)(2,1)S(1)}, bf16[2,2,2,2,2,2,16,1280]{7,6,1,0,5,4,3,2:T(8,128)(2,1)S(1)}, u32[]{:S(2)}, u32[]{:S(2)}) collective-permute-start(bf16[2,2,2,2,2,2,16,1280]{7,6,1,0,5,4,3,2:T(8,128)(2,1)S(1)} %pad_maximum_fusion.2), channel_id=1, source_target_pairs={{0,32},{1,33},{2,34},{3,35},{4,36},{5,37},{6,38},{7,39},{8,40},{9,... | collective-permute-start | bytes 7864328 | tf_op jit(solution)/shard_map/ppermute | solution.py:34
  104.2 25.0 %collective-permute-start.18 = (bf16[2,2,2,2,2,2,16,1280]{7,6,5,4,3,2,1,0:T(8,128)(2,1)S(1)}, bf16[2,2,2,2,2,2,16,1280]{7,6,5,4,3,2,1,0:T(8,128)(2,1)S(1)}, u32[]{:S(2)}, u32[]{:S(2)}) collective-permute-start(bf16[2,2,2,2,2,2,16,1280]{7,6,5,4,3,2,1,0:T(8,128)(2,1)S(1)} %pad_maximum_fusion), channel_id=1, source_target_pairs={{0,32},{1,33},{2,34},{3,35},{4,36},{5,37},{6,38},{7,39},{8,40},{9,... | collective-permute-start | bytes 7864328 | tf_op jit(solution)/shard_map/ppermute | solution.py:34
  124.1 92.3 %collective-permute-start.27 = (bf16[2,2,2,2,2,2,16,1280]{7,6,5,4,3,2,1,0:T(8,128)(2,1)}, bf16[2,2,2,2,2,2,16,1280]{7,6,5,4,3,2,1,0:T(8,128)(2,1)}, u32[]{:S(2)}, u32[]{:S(2)}) collective-permute-start(bf16[2,2,2,2,2,2,16,1280]{7,6,5,4,3,2,1,0:T(8,128)(2,1)} %pad_maximum_fusion.3), channel_id=1, source_target_pairs={{0,32},{1,33},{2,34},{3,35},{4,36},{5,37},{6,38},{7,39},{8,40},{9,... | collective-permute-start | bytes 7864328 | tf_op jit(solution)/shard_map/ppermute | solution.py:34
  209.0 49.8 %all-to-all-start = ((bf16[32,8,1440]{2,1,0:T(8,128)(2,1)}), bf16[32,8,1440]{2,1,0:T(8,128)(2,1)}, u32[]{:S(2)}, u32[]{:S(2)}) async-start(bf16[32,8,1440]{2,1,0:T(8,128)(2,1)} %bitcast.379), calls=%async_computation | async-start | bytes 1572864 | tf_op jit(solution)/shard_map/all_to_all | solution.py:184
  358.5 24.8 %all-to-all-start.2 = ((bf16[32,8,480]{2,1,0:T(8,128)(2,1)}), bf16[32,8,480]{2,1,0:T(8,128)(2,1)}, u32[]{:S(2)}, u32[]{:S(2)}) async-start(bf16[32,8,480]{2,1,0:T(8,128)(2,1)} %bitcast.86), calls=%async_computation.2 | async-start | bytes 524288 | tf_op jit(solution)/shard_map/all_to_all | solution.py:184
  381.0 95.8 %collective-permute-start.33 = (bf16[1024,1280]{0,1:T(8,128)(2,1)}, bf16[1024,1280]{0,1:T(8,128)(2,1)}, u32[]{:S(2)}, u32[]{:S(2)}) collective-permute-start(bf16[1024,1280]{0,1:T(8,128)(2,1)} %pad_maximum_fusion.7), channel_id=1, source_target_pairs={{0,32},{1,33},{2,34},{3,35},{4,36},{5,37},{6,38},{7,39},{8,40},{9,... | collective-permute-start | bytes 7864328 | tf_op jit(solution)/shard_map/ppermute | solution.py:34
  382.8 101.9 %collective-permute-start.43 = (bf16[1024,1280]{0,1:T(8,128)(2,1)}, bf16[1024,1280]{0,1:T(8,128)(2,1)}, u32[]{:S(2)}, u32[]{:S(2)}) collective-permute-start(bf16[1024,1280]{0,1:T(8,128)(2,1)} %pad_maximum_fusion.9), channel_id=1, source_target_pairs={{0,32},{1,33},{2,34},{3,35},{4,36},{5,37},{6,38},{7,39},{8,40},{9,... | collective-permute-start | bytes 7864328 | tf_op jit(solution)/shard_map/ppermute | solution.py:34
  396.0 25.5 %all-to-all-start.3 = ((bf16[32,8,1440]{2,1,0:T(8,128)(2,1)}), bf16[32,8,1440]{2,1,0:T(8,128)(2,1)}, u32[]{:S(2)}, u32[]{:S(2)}) async-start(bf16[32,8,1440]{2,1,0:T(8,128)(2,1)} %concatenate.158), calls=%async_computation.3 | async-start | bytes 1572864 | tf_op jit(solution)/shard_map/all_to_all | solution.py:187
  409.4 96.3 %collective-permute-start.53 = (bf16[1024,1280]{0,1:T(8,128)(2,1)}, bf16[1024,1280]{0,1:T(8,128)(2,1)}, u32[]{:S(2)}, u32[]{:S(2)}) collective-permute-start(bf16[1024,1280]{0,1:T(8,128)(2,1)} %pad_maximum_fusion.11), channel_id=1, source_target_pairs={{0,32},{1,33},{2,34},{3,35},{4,36},{5,37},{6,38},{7,39},{8,40},{9,... | collective-permute-start | bytes 7864328 | tf_op jit(solution)/shard_map/ppermute | solution.py:34
  472.8 44.6 %collective-permute-start.30 = (bf16[1024,1280]{0,1:T(8,128)(2,1)}, bf16[1024,1280]{0,1:T(8,128)(2,1)}, u32[]{:S(2)}, u32[]{:S(2)}) collective-permute-start(bf16[1024,1280]{0,1:T(8,128)(2,1)} %pad_maximum_fusion.6), channel_id=1, source_target_pairs={{0,32},{1,33},{2,34},{3,35},{4,36},{5,37},{6,38},{7,39},{8,40},{9,... | collective-permute-start | bytes 7864328 | tf_op jit(solution)/shard_map/ppermute | solution.py:34
  474.6 50.9 %collective-permute-start.40 = (bf16[1024,1280]{0,1:T(8,128)(2,1)}, bf16[1024,1280]{0,1:T(8,128)(2,1)}, u32[]{:S(2)}, u32[]{:S(2)}) collective-permute-start(bf16[1024,1280]{0,1:T(8,128)(2,1)} %pad_maximum_fusion.8), channel_id=1, source_target_pairs={{0,32},{1,33},{2,34},{3,35},{4,36},{5,37},{6,38},{7,39},{8,40},{9,... | collective-permute-start | bytes 7864328 | tf_op jit(solution)/shard_map/ppermute | solution.py:34
  476.8 67.6 %collective-permute-start.50 = (bf16[1024,1280]{0,1:T(8,128)(2,1)}, bf16[1024,1280]{0,1:T(8,128)(2,1)}, u32[]{:S(2)}, u32[]{:S(2)}) collective-permute-start(bf16[1024,1280]{0,1:T(8,128)(2,1)} %pad_maximum_fusion.10), channel_id=1, source_target_pairs={{0,32},{1,33},{2,34},{3,35},{4,36},{5,37},{6,38},{7,39},{8,40},{9,... | collective-permute-start | bytes 7864328 | tf_op jit(solution)/shard_map/ppermute | solution.py:34
  484.7 69.4 %collective-permute-start.34 = (bf16[2,2,2,2,2,16,1280]{6,5,4,3,2,1,0:T(8,128)(2,1)}, bf16[2,2,2,2,2,16,1280]{6,5,4,3,2,1,0:T(8,128)(2,1)}, u32[]{:S(2)}, u32[]{:S(2)}) collective-permute-start(bf16[2,2,2,2,2,16,1280]{6,5,4,3,2,1,0:T(8,128)(2,1)} %bitcast.399), channel_id=1, source_target_pairs={{0,80},{1,81},{2,82},{3,83},{4,84},{5,85},{6,86},{7,87},{8,88},{9,... | collective-permute-start | bytes 3932168 | tf_op jit(solution)/shard_map/ppermute | solution.py:30
  505.7 51.8 %collective-permute-start.44 = (bf16[2,2,2,2,2,16,1280]{6,5,3,2,1,0,4:T(8,128)(2,1)}, bf16[2,2,2,2,2,16,1280]{6,5,3,2,1,0,4:T(8,128)(2,1)}, u32[]{:S(2)}, u32[]{:S(2)}) collective-permute-start(bf16[2,2,2,2,2,16,1280]{6,5,3,2,1,0,4:T(8,128)(2,1)} %bitcast.341), channel_id=1, source_target_pairs={{0,3},{1,2},{2,1},{3,0},{4,7},{5,6},{6,5},{7,4},{8,11},{9,10},{10,... | collective-permute-start | bytes 3932168 | tf_op jit(solution)/shard_map/ppermute | solution.py:30
  517.4 43.3 %collective-permute-start.54 = (bf16[2,2,2,2,2,16,1280]{6,5,1,0,4,3,2:T(8,128)(2,1)}, bf16[2,2,2,2,2,16,1280]{6,5,1,0,4,3,2:T(8,128)(2,1)}, u32[]{:S(2)}, u32[]{:S(2)}) collective-permute-start(bf16[2,2,2,2,2,16,1280]{6,5,1,0,4,3,2:T(8,128)(2,1)} %bitcast.339), channel_id=1, source_target_pairs={{0,12},{1,13},{2,14},{3,15},{4,8},{5,9},{6,10},{7,11},{8,4},{9,5},... | collective-permute-start | bytes 3932168 | tf_op jit(solution)/shard_map/ppermute | solution.py:30
  525.4 53.7 %collective-permute-start.31 = (bf16[2,2,2,2,2,16,1280]{6,5,4,3,2,1,0:T(8,128)(2,1)}, bf16[2,2,2,2,2,16,1280]{6,5,4,3,2,1,0:T(8,128)(2,1)}, u32[]{:S(2)}, u32[]{:S(2)}) collective-permute-start(bf16[2,2,2,2,2,16,1280]{6,5,4,3,2,1,0:T(8,128)(2,1)} %bitcast.400), channel_id=1, source_target_pairs={{0,80},{1,81},{2,82},{3,83},{4,84},{5,85},{6,86},{7,87},{8,88},{9,... | collective-permute-start | bytes 3932168 | tf_op jit(solution)/shard_map/ppermute | solution.py:30
  544.4 37.9 %collective-permute-start.41 = (bf16[2,2,2,2,2,16,1280]{6,5,3,2,1,0,4:T(8,128)(2,1)}, bf16[2,2,2,2,2,16,1280]{6,5,3,2,1,0,4:T(8,128)(2,1)}, u32[]{:S(2)}, u32[]{:S(2)}) collective-permute-start(bf16[2,2,2,2,2,16,1280]{6,5,3,2,1,0,4:T(8,128)(2,1)} %bitcast.342), channel_id=1, source_target_pairs={{0,3},{1,2},{2,1},{3,0},{4,7},{5,6},{6,5},{7,4},{8,11},{9,10},{10,... | collective-permute-start | bytes 3932168 | tf_op jit(solution)/shard_map/ppermute | solution.py:30
  554.1 30.1 %collective-permute-start.51 = (bf16[2,2,2,2,2,16,1280]{6,5,1,0,4,3,2:T(8,128)(2,1)S(1)}, bf16[2,2,2,2,2,16,1280]{6,5,1,0,4,3,2:T(8,128)(2,1)S(1)}, u32[]{:S(2)}, u32[]{:S(2)}) collective-permute-start(bf16[2,2,2,2,2,16,1280]{6,5,1,0,4,3,2:T(8,128)(2,1)S(1)} %bitcast.401), channel_id=1, source_target_pairs={{0,12},{1,13},{2,14},{3,15},{4,8},{5,9},{6,10},{7,11},{8,4},{9,5},... | collective-permute-start | bytes 3932168 | tf_op jit(solution)/shard_map/ppermute | solution.py:30
  (118 other events, 1975.9 us)
